TPU v7x, 32 devices: a whole 2x2x4 slice. The times are simulated.
32 devices in a mesh: grp: 2 (over x), wide: 16 (over z, y, core).
Axes of the slice: x: 2, y: 2, z: 4, core: 2. Of those that a mesh axis runs over, the one named last changes fastest.
Arguments:
- xblocks: bfloat16 [128, 64, 64], P(('grp', 'wide')), parts along dimension 0, may hold values from -6 to 6
- pattern: int32 [3, 128], P(None, ('grp', 'wide')), parts along dimension 1, may hold values from 0 to 31, as said below
- counts: int32 [32], P(('grp', 'wide')), parts along dimension 0, may hold values from 1 to 4, as said below
- coef: bfloat16 [2048, 4096], P(None, 'wide'), may hold values from -0.25 to 0.25
Outputs:
- features: bfloat16 [16, 4096, 4096], P('grp', 'wide'), parts along dimension 0
There are 2 independent parts, one for each index of `grp`. A program takes and returns all parts, laid end to end along the dimension named above; an argument that names none is the same for every part. Nothing has to cross between parts.
Inputs may be any that keep to these rules, and one draw needn't show every extreme that they name: pattern[0] is the pair (below 8), pattern[1] and pattern[2] the bra and ket AO blocks (below 32); no triple occurs twice. `counts`: slots at and after a device's count are not part of the problem.
All inputs are finite; a program needn't handle non-finite values.
Results may differ from a plain program's by a relative error of at most 0.0051.
Values may be sent and summed in bfloat16 or wider, within the bound.
A program may use at most 128 MiB of HBM per device.

v0:
```python
import jax
import jax.numpy as jnp
from jax import lax
from jax.sharding import PartitionSpec as P

DOMAIN_BLOCKS = 32
PAIR_COUNT = 8


def local(xblocks, pattern, counts, coef):
    slot_count = xblocks.shape[0]
    block_tile = xblocks.shape[1]
    column_list = coef.shape[1]
    targets_all = PAIR_COUNT * DOMAIN_BLOCKS
    active_mask = jnp.arange(slot_count, dtype=jnp.int32) < counts[0]
    destination = jnp.where(active_mask, pattern[0] * DOMAIN_BLOCKS + pattern[1], -1)
    local_rows = coef.reshape(DOMAIN_BLOCKS, block_tile, column_list)
    blocks = lax.all_gather(xblocks, "wide", axis=0, tiled=True)
    tgt = lax.all_gather(destination, "wide", axis=0, tiled=True)
    sigma = lax.all_gather(pattern[2], "wide", axis=0, tiled=True)
    picked = local_rows[sigma]
    contribution = jnp.einsum(
        "sij,sjb->sib", blocks, picked, preferred_element_type=jnp.float32
    ).astype(jnp.bfloat16)
    flattened = contribution.reshape(blocks.shape[0], block_tile * column_list)
    selector = (tgt[None, :] == jnp.arange(targets_all, dtype=jnp.int32)[:, None]).astype(
        jnp.bfloat16
    )
    half_sum = jnp.dot(selector, flattened, preferred_element_type=jnp.float32)
    half = half_sum.astype(jnp.bfloat16).reshape(
        PAIR_COUNT, DOMAIN_BLOCKS * block_tile, column_list
    )
    return jnp.einsum(
        "pnb,na->pba",
        half,
        lax.all_gather(coef, "wide", axis=1, tiled=True),
        preferred_element_type=jnp.float32,
    ).astype(jnp.bfloat16)


def solution(mesh):
    placed = (
        P(("grp", "wide"), None, None),
        P(None, ("grp", "wide")),
        P(("grp", "wide")),
        P(None, "wide"),
    )
    return jax.shard_map(
        local, mesh=mesh, in_specs=placed, out_specs=P("grp", "wide", None), check_vma=False
    )
```

profile of v0, /device:TPU:1, one launch (start us, length us, event | category | flops | bytes accessed | tf_op | source)
XLA Modules:
  0.0 199.8 jit_solution(9037635594761458630)
XLA Ops:
  6.5 0.0 all-gather.3.cloned.1.call-start
  6.5 0.7 all-gather.3.cloned.1.call-update
  7.9 1.2 dynamic-slice
  9.8 0.8 bitcast_dynamic-update-slice_fusion
  10.6 0.8 fusion.6
  11.4 10.7 %all-reduce.2 = (s32[64]{0:T(128)S(1)}, s32[64]{0:T(128)S(1)}) all-reduce(s32[64]{0:T(128)S(1)} %bitcast_dynamic-update-slice_fusion, s32[64]{0:T(128)S(1)} %fusion.6), channel_id=2, replica_groups=mesh['grp'=2,'wide'=16] {'wide'}, use_global_device_ids=true, to_apply=%add.1 | all-reduce | flops 128 | bytes 1024 | tf_op jit(solution)/shard_map/all_gather | solution.py:20
  22.1 1.9 gather_fusion
  24.1 29.6 %all_gather.14 = bf16[64,64,64]{2,1,0:T(8,128)(2,1)S(1)} all-gather(bf16[4,64,64]{2,1,0:T(8,128)(2,1)} %param.4), channel_id=1, replica_groups=mesh['grp'=2,'wide'=16] {'wide'}, dimensions={0}, use_global_device_ids=true | all-gather | bytes 557056 | tf_op jit(solution)/shard_map/all_gather | solution.py:18
  53.7 0.7 convolution_convert_fusion.1
  54.4 1.3 copy.8
  55.7 5.7 %convolution_convert_fusion = bf16[256,16384]{1,0:T(8,128)(2,1)} fusion(bf16[64,16384]{1,0:T(8,128)(2,1)S(1)} %bitcast.22, s32[64]{0:T(128)S(1)} %get-tuple-element.6), kind=kOutput, calls=%fused_computation.1 | convolution fusion | flops 541081600 | bytes 10486016 | tf_op jit(solution)/shard_map/dot_general | solution.py:29
  61.4 13.7 %reshape.15 = bf16[8,2048,256]{2,1,0:T(8,128)(2,1)} reshape(bf16[256,16384]{1,0:T(8,128)(2,1)} %convolution_convert_fusion) | data formatting | bytes 16777216 | tf_op jit(solution)/shard_map/reshape | solution.py:30
  75.1 75.9 %all-gather.3.cloned.1.call-done = bf16[2048,4096]{1,0:T(8,128)(2,1)} async-done(((bf16[2048,256]{1,0:T(8,128)(2,1)}), bf16[2048,4096]{1,0:T(8,128)(2,1)}) %all-gather.3.cloned.1.call-update) | async-done | bytes 16777232 | tf_op jit(solution)/shard_map/all_gather | solution.py:36
  151.0 42.0 %fusion.2 = bf16[8,256,4096]{2,1,0:T(8,128)(2,1)} fusion(bf16[8,2048,256]{2,1,0:T(8,128)(2,1)} %reshape.15, bf16[2048,4096]{1,0:T(8,128)(2,1)} %all-gather.3.cloned.1.call-done), kind=kOutput, calls=%fused_computation.4 | convolution fusion | flops 34368126976 | bytes 41943040 | tf_op jit(solution)/shard_map/pnb,na->pba/dot_general | solution.py:33
  (4 shorter events, 0.0 us)
Async XLA Ops:
  6.5 144.5 %all-gather.3.cloned.1.call-start = ((), (), s32[]{:S(2)}) async-start(), calls=%async_computation | async-start | bytes 17825792 | tf_op jit(solution)/shard_map/all_gather | solution.py:36
Sparse Core Ops, SparseCore 0:
  9.5 141.4 all-gather.2
where the time goes:
time: 201 us; the launch traced here: 200 us
  waiting for transfers between devices  76.6 us (38%)
  matrix products  48.4 us (24%)
  blocking collectives  40.3 us (20%)
  local copies, waits for them, and re-layouts  18.9 us (9%)
  between operations  14.7 us (7%)
    all_gather x1, waiting for transfers between devices, local(): lax.all_gather(coef, 'wide', axis=1, tiled=True)  75.9 us
    dot_general x1, matrix products, local(): jnp.einsum('pnb,na->pba', half, lax.all_gather(coef, 'wide', axis=1, tile...  42 us
    all_gather x1, blocking collectives, local(): blocks = lax.all_gather(xblocks, 'wide', axis=0, tiled=True)  29.6 us
    reshape x1, local copies, waits for them, and re-layouts, local(): half_sum.astype(jnp.bfloat16)  13.7 us
    all_gather x1, blocking collectives, local(): sigma = lax.all_gather(pattern[2], 'wide', axis=0, tiled=True)  10.7 us
    dot_general x1, matrix products, local(): half_sum = jnp.dot(selector, flattened, preferred_element_type=jnp.float32)  5.71 us
  transfers between devices with their start and end apart: 1, of which 1 were waited for; matrix products, arithmetic and copies ran while one was open for 13% of the time, Pallas kernels for 0%

commit v1 on v0

--- a/solution.py
+++ b/solution.py
@@ -1,13 +1,354 @@
+import functools
+
 import jax
 import jax.numpy as jnp
 from jax import lax
+from jax.experimental import pallas as pl
+from jax.experimental.pallas import tpu as pltpu
 from jax.sharding import PartitionSpec as P
 
 DOMAIN_BLOCKS = 32
 PAIR_COUNT = 8
-
-
-def local(xblocks, pattern, counts, coef):
+MESH = pl.DeviceIdType.MESH
+PAYLOAD = 4
+CHUNKS = 5
+UP, DOWN, Y, X, CORE = range(5)
+
+
+def gather_kernel(nz, coef_ref, pay_ref, full_ref, pays_ref, send_sem, recv_sem, local_sem):
+    x = lax.axis_index("grp")
+    wide = lax.axis_index("wide")
+    z, y, core = lax.div(wide, 4), lax.rem(lax.div(wide, 2), 2), lax.rem(wide, 2)
+    other = 1 - y
+    quarter = coef_ref.shape[0] // 4
+
+    def index(zz, yy, cc):
+        return (zz * 2 + yy) * 2 + cc
+
+    device = {
+        UP: {"wide": wide + 4},
+        DOWN: {"wide": wide - 4},
+        Y: {"wide": index(z, 1 - y, core)},
+        X: {"grp": 1 - x},
+        CORE: {"wide": index(z, y, 1 - core)},
+    }
+    barrier = pltpu.get_barrier_semaphore()
+    for to in (Y, X, CORE):
+        pl.semaphore_signal(barrier, inc=1, device_id=device[to], device_id_type=MESH)
+
+    @pl.when(z < nz - 1)
+    def _():
+        pl.semaphore_signal(barrier, inc=1, device_id=device[UP], device_id_type=MESH)
+
+    @pl.when(z > 0)
+    def _():
+        pl.semaphore_signal(barrier, inc=1, device_id=device[DOWN], device_id_type=MESH)
+
+    inner = (z > 0).astype(jnp.int32) + (z < nz - 1).astype(jnp.int32)
+    pl.semaphore_wait(barrier, 3 + inner)
+
+    def ref_of(w, q, own=False):
+        if isinstance(q, int) and q == PAYLOAD:
+            return pay_ref if own else pays_ref.at[w]
+        rows = pl.ds(pl.multiple_of(q * quarter, quarter), quarter)
+        return coef_ref.at[rows] if own else full_ref.at[w, rows]
+
+    def copy(to, zz, yy, q, own=False):
+        w = index(zz, yy, core)
+        return pltpu.make_async_remote_copy(
+            src_ref=ref_of(w, q, own),
+            dst_ref=ref_of(w, q),
+            send_sem=send_sem.at[to, (zz * 2 + yy) * CHUNKS + q],
+            recv_sem=recv_sem.at[w * CHUNKS + q],
+            device_id=device[to],
+            device_id_type=MESH,
+        )
+
+    sent = []
+
+    def send(to, zz, yy, q, own=False, when=None):
+        sent.append((to, zz, yy, q, own, when))
+        copy(to, zz, yy, q, own).start()
+
+    def arrived(w, q):
+        pltpu.make_async_remote_copy(
+            src_ref=ref_of(w, q),
+            dst_ref=ref_of(w, q),
+            send_sem=send_sem.at[CORE, 0],
+            recv_sem=recv_sem.at[w * CHUNKS + q],
+            device_id=device[CORE],
+            device_id_type=MESH,
+        ).wait_recv()
+
+    def guarded(when, body):
+        if when is None:
+            body()
+        else:
+            pl.when(when)(body)
+
+    first, second, third, missing = 3 * x, 1 + x, 2 - x, 3 - 3 * x
+    along_z = (PAYLOAD, first, second, third)
+
+    for q in along_z:
+        for to, when in ((UP, z < nz - 1), (DOWN, z > 0)):
+            guarded(when, functools.partial(send, to, z, y, q, True, when))
+    for q in (PAYLOAD, first, second, third, missing):
+        send(Y, z, y, q, True)
+        send(CORE, z, y, q, True)
+    mine = [
+        pltpu.make_async_copy(coef_ref, full_ref.at[wide], local_sem.at[0]),
+        pltpu.make_async_copy(pay_ref, pays_ref.at[wide], local_sem.at[1]),
+    ]
+    for c in mine:
+        c.start()
+
+    def sides(d):
+        return ((z - d, z >= d, UP, z < nz - 1), (z + d, z + d < nz, DOWN, z > 0))
+
+    def take_z(d):
+        for q in along_z:
+            for zz, valid, onward, more in sides(d):
+                both = jnp.logical_and(valid, more)
+
+                def body(zz=zz, valid=valid, onward=onward, both=both, q=q):
+                    arrived(index(zz, y, core), q)
+                    if d < nz - 1:
+                        guarded(both, functools.partial(send, onward, zz, y, q, False, both))
+                    if q is not third:
+                        send(Y, zz, y, q, False, valid)
+                    if q is first:
+                        send(X, zz, y, q, False, valid)
+                    send(CORE, zz, y, q, False, valid)
+
+                guarded(valid, body)
+
+    def take_y_own():
+        for q in (PAYLOAD, first, second, third, missing):
+            arrived(index(z, other, core), q)
+            send(CORE, z, other, q)
+
+    def take_y(d):
+        for q in (PAYLOAD, first, second):
+            for zz, valid, _, _ in sides(d):
+
+                def body(zz=zz, valid=valid, q=q):
+                    arrived(index(zz, other, core), q)
+                    if q is not PAYLOAD:
+                        send(X, zz, other, q, False, valid)
+                    send(CORE, zz, other, q, False, valid)
+
+                guarded(valid, body)
+
+    def take_x(d):
+        for yy, q in ((y, missing), (other, missing), (other, third)):
+            for zz, valid, _, _ in sides(d):
+
+                def body(zz=zz, valid=valid, q=q, yy=yy):
+                    arrived(index(zz, yy, core), q)
+                    send(CORE, zz, yy, q, False, valid)
+
+                guarded(valid, body)
+
+    for step in range(1, nz + 2):
+        if step < nz:
+            take_z(step)
+        if step == 1:
+            take_y_own()
+        elif step - 1 < nz:
+            take_y(step - 1)
+        if 1 <= step - 2:
+            take_x(step - 2)
+
+    for zz in range(nz):
+        for yy in range(2):
+            for q in range(CHUNKS):
+                arrived(index(zz, yy, 1 - core), q)
+    for c in mine:
+        c.wait()
+    for to, zz, yy, q, own, when in sent:
+        guarded(when, lambda: copy(to, zz, yy, q, own).wait_send())
+
+
+def gather(coef, payload, wide):
+    rows, columns = coef.shape
+    nz = wide // 4
+    return pl.pallas_call(
+        functools.partial(gather_kernel, nz),
+        out_shape=(
+            jax.ShapeDtypeStruct((wide, rows, columns), coef.dtype),
+            jax.ShapeDtypeStruct((wide,) + payload.shape, payload.dtype),
+        ),
+        in_specs=[pl.BlockSpec(memory_space=pl.ANY)] * 2,
+        out_specs=(pl.BlockSpec(memory_space=pl.ANY),) * 2,
+        scratch_shapes=[
+            pltpu.SemaphoreType.DMA((5, nz * 2 * CHUNKS)),
+            pltpu.SemaphoreType.DMA((wide * CHUNKS,)),
+            pltpu.SemaphoreType.DMA((2,)),
+        ],
+        compiler_params=pltpu.CompilerParams(collective_id=0, has_side_effects=True),
+        cost_estimate=pl.CostEstimate(
+            flops=0, bytes_accessed=2 * wide * rows * columns * 2, transcendentals=0
+        ),
+    )(coef, payload)
+
+
+def product_kernel(
+    block, meta, pays_ref, coef_ref, full_ref, out_ref, half_ref, acc_ref, place, bra_of, start, fill
+):
+    slots = meta.shape[0] * 4
+    places = place.shape[0]
+
+    @pl.when(pl.program_id(0) == 0)
+    def _():
+        def clear(i, _):
+            place[i] = -1
+            bra_of[i] = 0
+            return 0
+
+        lax.fori_loop(0, places, clear, 0)
+        for p in range(PAIR_COUNT):
+            fill[p] = 0
+
+        def count(s, _):
+            w, r = s // 4, s % 4
+
+            @pl.when(meta[w, 12 + r] > 0)
+            def _():
+                p = meta[w, r]
+                fill[p] = fill[p] + 1
+
+            return 0
+
+        lax.fori_loop(0, slots, count, 0)
+        start[0] = 0
+        for p in range(PAIR_COUNT):
+            start[p + 1] = start[p] + (fill[p] + 3) // 4
+            fill[p] = 4 * start[p]
+
+        def put(s, _):
+            w, r = s // 4, s % 4
+
+            @pl.when(meta[w, 12 + r] > 0)
+            def _():
+                p = meta[w, r]
+                to = fill[p]
+                place[to] = s
+                bra_of[to] = meta[w, 4 + r]
+                fill[p] = to + 1
+
+            return 0
+
+        lax.fori_loop(0, slots, put, 0)
+
+        def make(g, _):
+            parts = []
+            for k in range(4):
+                s = place[4 * g + k]
+                at = jnp.maximum(s, 0)
+                w, r = at // 4, at % 4
+                two = pays_ref[w, pl.ds(pl.multiple_of((r // 2) * block, block), block), :]
+                one = jnp.where(r % 2 == 0, two[:, :block], two[:, block:])
+                one = jnp.where(s >= 0, one, jnp.zeros_like(one))
+                ket = meta[w, 8 + r]
+                rows = coef_ref[pl.ds(pl.multiple_of(ket * block, block), block), :]
+                parts.append(jnp.dot(one, rows, preferred_element_type=jnp.float32))
+            half_ref[g] = jnp.concatenate(parts, axis=0).T.astype(jnp.bfloat16)
+            return 0
+
+        lax.fori_loop(0, start[PAIR_COUNT], make, 0)
+
+    tiles = full_ref.shape[0]
+    width = full_ref.shape[2]
+
+    def term(t, g):
+        rows = [
+            full_ref[t, pl.ds(pl.multiple_of(bra_of[4 * g + k] * block, block), block), :]
+            for k in range(4)
+        ]
+        return jnp.dot(
+            half_ref[g], jnp.concatenate(rows, axis=0), preferred_element_type=jnp.float32
+        )
+
+    for p in range(PAIR_COUNT):
+        begin = start[p]
+        groups = start[p + 1] - begin
+
+        @pl.when(groups == 0)
+        def _():
+            out_ref[p] = jnp.zeros(out_ref.shape[1:], out_ref.dtype)
+
+        @pl.when(groups == 1)
+        def _():
+            for t in range(tiles):
+                out_ref[p, :, t * width : (t + 1) * width] = term(t, begin).astype(out_ref.dtype)
+
+        @pl.when(groups == 2)
+        def _():
+            for t in range(tiles):
+                out_ref[p, :, t * width : (t + 1) * width] = (
+                    term(t, begin) + term(t, begin + 1)
+                ).astype(out_ref.dtype)
+
+        @pl.when(groups > 2)
+        def _():
+            for t in range(tiles):
+                acc_ref[...] = term(t, begin)
+
+                def more(g, _, t=t):
+                    acc_ref[...] += term(t, g)
+                    return 0
+
+                lax.fori_loop(begin + 1, begin + groups, more, 0)
+                out_ref[p, :, t * width : (t + 1) * width] = acc_ref[...].astype(out_ref.dtype)
+
+
+def product(meta, pays, coef, full, block):
+    wide, rows, columns = full.shape
+    tiles = 2
+    most = wide + PAIR_COUNT
+    return pl.pallas_call(
+        functools.partial(product_kernel, block),
+        out_shape=jax.ShapeDtypeStruct((PAIR_COUNT, columns, wide * columns), jnp.bfloat16),
+        grid_spec=pltpu.PrefetchScalarGridSpec(
+            num_scalar_prefetch=1,
+            grid=(wide // tiles,),
+            in_specs=[
+                pl.BlockSpec(pays.shape, lambda i, m: (0, 0, 0)),
+                pl.BlockSpec(coef.shape, lambda i, m: (0, 0)),
+                pl.BlockSpec((tiles, rows, columns), lambda i, m: (i, 0, 0)),
+            ],
+            out_specs=pl.BlockSpec(
+                (PAIR_COUNT, columns, tiles * columns), lambda i, m: (0, 0, i)
+            ),
+            scratch_shapes=[
+                pltpu.VMEM((most, columns, 4 * block), jnp.bfloat16),
+                pltpu.VMEM((columns, columns), jnp.float32),
+                pltpu.SMEM((4 * most,), jnp.int32),
+                pltpu.SMEM((4 * most,), jnp.int32),
+                pltpu.SMEM((PAIR_COUNT + 1,), jnp.int32),
+                pltpu.SMEM((PAIR_COUNT,), jnp.int32),
+            ],
+        ),
+        compiler_params=pltpu.CompilerParams(vmem_limit_bytes=48 * 1024 * 1024),
+    )(meta, pays, coef, full)
+
+
+def local(wide, xblocks, pattern, counts, coef):
+    slots, block, _ = xblocks.shape
+    live = (jnp.arange(slots, dtype=jnp.int32) < counts[0]).astype(jnp.int32)
+    numbers = jnp.concatenate([pattern, live[None]], axis=0).astype(jnp.bfloat16)
+    pairs = xblocks.reshape(slots // 2, 2, block, block).transpose(0, 2, 1, 3)
+    pairs = pairs.reshape(slots // 2 * block, 2 * block)
+    payload = jnp.concatenate(
+        [pairs, jnp.pad(numbers, ((0, 12), (0, 2 * block - slots)))], axis=0
+    )
+    full, pays = gather(coef, payload, wide)
+    at = slots // 2 * block
+    meta = pays[:, at : at + 4, :slots].astype(jnp.int32).reshape(wide, 4 * slots)
+    return product(meta, pays, coef, full, block)
+
+
+def local_any(xblocks, pattern, counts, coef):
     slot_count = xblocks.shape[0]
     block_tile = xblocks.shape[1]
     column_list = coef.shape[1]
@@ -45,6 +386,8 @@
         P(("grp", "wide")),
         P(None, "wide"),
     )
+    wide = mesh.shape["wide"]
+    body = functools.partial(local, wide) if wide == 16 and mesh.shape["grp"] == 2 else local_any
     return jax.shard_map(
-        local, mesh=mesh, in_specs=placed, out_specs=P("grp", "wide", None), check_vma=False
-    )
+        body, mesh=mesh, in_specs=placed, out_specs=P("grp", "wide", None), check_vma=False
+    )

time: 201 us -> 121 us (0.60)
  Pallas kernels: 0 us -> 115 us
  waiting for transfers between devices: 76.6 us -> 0 us
  matrix products: 48.4 us -> 0 us
  blocking collectives: 40.3 us -> 0 us
  local copies, waits for them, and re-layouts: 18.9 us -> 3.48 us
  between operations: 14.7 us -> 0.68 us
    pallas_call x0 -> x2, Pallas kernels: none -> 115 us  [the longest x1 86.5 us: gather(): pl.pallas_call(functools.partial(gather_kernel, nz), out_shape=(jax.Shape...]
    all_gather x1 -> x0, waiting for transfers between devices: 75.9 us -> none  [local(): lax.all_gather(coef, 'wide', axis=1, tiled=True)]
    dot_general x3 -> x0, matrix products: 48.4 us -> none  [the longest x1 42 us: local(): jnp.einsum('pnb,na->pba', half, lax.all_gather(coef, 'wide', axis=1, tile...]
    all_gather x2 -> x0, blocking collectives: 40.3 us -> none  [the longest x1 29.6 us: local(): blocks = lax.all_gather(xblocks, 'wide', axis=0, tiled=True)]
    reshape x1 -> x4, local copies, waits for them, and re-layouts: 13.7 us -> 1.18 us  [the longest x1 0.91 us: local(): pairs = xblocks.reshape(slots // 2, 2, block, block).transpose(0, 2, 1, 3)]
  transfers between devices with their start and end apart: 1 -> 0, of which waited for: 1 -> 0; matrix products, arithmetic and copies ran while one was open for 13% -> 0% of each run, Pallas kernels for 0% -> 0%
where the time goes in v1:
time: 121 us
  Pallas kernels  115 us (95%)
  local copies, waits for them, and re-layouts  3.48 us (3%)
  other arithmetic  2.1 us (2%)
    pallas_call x1, Pallas kernels, gather(): pl.pallas_call(functools.partial(gather_kernel, nz), out_shape=(jax.Shape...  86.5 us
    pallas_call x1, Pallas kernels, product(): pl.pallas_call(functools.partial(product_kernel, block), out_shape=jax.Sh...  28.4 us

profile of v1, /device:TPU:1, one launch (start us, length us, event | category | flops | bytes accessed | tf_op | source)
XLA Modules:
  0.0 121.1 jit_solution(10759681349030834529)
XLA Ops:
  0.7 0.7 convert.7
  1.4 0.9 copy.13
  2.3 0.1 reshape.22
  2.4 0.6 pad_maximum_fusion.pay_ref
  3.0 86.5 %shard_map.46 = (bf16[16,2048,256]{2,1,0:T(8,128)(2,1)}, bf16[16,144,128]{2,1,0:T(8,128)(2,1)}) custom-call(bf16[2048,256]{1,0:T(8,128)(2,1)} %coef_ref.3, bf16[144,128]{1,0:T(8,128)(2,1)} %pad_maximum_fusion.pay_ref), custom_call_target="tpu_custom_call" | custom-call | bytes 33554432 | tf_op jit(solution)/shard_map/pallas_call | solution.py:175
  89.5 0.8 slice_convert_fusion
  90.2 0.1 copy.10
  90.4 0.1 copy.11.meta
  90.4 0.0 copy-start
  90.4 1.2 %copy-done = bf16[2048,256]{1,0:T(8,128)(2,1)S(1)} copy-done((bf16[2048,256]{1,0:T(8,128)(2,1)S(1)}, bf16[2048,256]{1,0:T(8,128)(2,1)}, u32[]{:S(2)}) %copy-start) | copy-done | bytes 1048600
  91.7 0.0 copy-start.1
  91.7 1.1 copy-done.1
  92.7 28.4 %shard_map.47 = bf16[8,256,4096]{2,1,0:T(8,128)(2,1)} custom-call(s32[16,16]{1,0:T(8,128)S(1)} %copy.11.meta, bf16[16,144,128]{2,1,0:T(8,128)(2,1)S(1)} %copy-done.1, bf16[2048,256]{1,0:T(8,128)(2,1)S(1)} %copy-done, bf16[16,2048,256]{2,1,0:T(8,128)(2,1)} %get-tuple-element.8.full_ref), custom_call_target="tpu_custom_call" | custom-call | tf_op jit(solution)/shard_map/pallas_call | solution.py:309
  (2 shorter events, 0.0 us)
Async XLA Ops:
  90.4 1.2 %copy-start = (bf16[2048,256]{1,0:T(8,128)(2,1)S(1)}, bf16[2048,256]{1,0:T(8,128)(2,1)}, u32[]{:S(2)}) copy-start(bf16[2048,256]{1,0:T(8,128)(2,1)} %coef_ref.3) | copy-start | bytes 3145732
  91.7 1.1 copy-start.1

commit v2 on v1

--- a/solution.py
+++ b/solution.py
@@ -64,10 +64,10 @@
             device_id_type=MESH,
         )
 
-    sent = []
-
-    def send(to, zz, yy, q, own=False, when=None):
-        sent.append((to, zz, yy, q, own, when))
+    sent, paced = [], []
+
+    def send(to, zz, yy, q, own=False, when=None, group=sent):
+        group.append((to, zz, yy, q, own, when))
         copy(to, zz, yy, q, own).start()
 
     def arrived(w, q):
@@ -87,13 +87,16 @@
             pl.when(when)(body)
 
     first, second, third, missing = 3 * x, 1 + x, 2 - x, 3 - 3 * x
-    along_z = (PAYLOAD, first, second, third)
-
-    for q in along_z:
+    early = (PAYLOAD, first, second)
+
+    def send_z(q):
         for to, when in ((UP, z < nz - 1), (DOWN, z > 0)):
             guarded(when, functools.partial(send, to, z, y, q, True, when))
+
+    for q in (PAYLOAD, first, second):
+        send_z(q)
+        send(Y, z, y, q, True)
     for q in (PAYLOAD, first, second, third, missing):
-        send(Y, z, y, q, True)
         send(CORE, z, y, q, True)
     mine = [
         pltpu.make_async_copy(coef_ref, full_ref.at[wide], local_sem.at[0]),
@@ -102,18 +105,23 @@
     for c in mine:
         c.start()
 
+    def settle(group):
+        for to, zz, yy, q, own, when in group:
+            guarded(when, lambda: copy(to, zz, yy, q, own).wait_send())
+
     def sides(d):
         return ((z - d, z >= d, UP, z < nz - 1), (z + d, z + d < nz, DOWN, z > 0))
 
-    def take_z(d):
-        for q in along_z:
+    def take_z(d, quarters):
+        for q in quarters:
             for zz, valid, onward, more in sides(d):
                 both = jnp.logical_and(valid, more)
 
                 def body(zz=zz, valid=valid, onward=onward, both=both, q=q):
                     arrived(index(zz, y, core), q)
                     if d < nz - 1:
-                        guarded(both, functools.partial(send, onward, zz, y, q, False, both))
+                        group = paced if d == 2 and q is not third else sent
+                        guarded(both, functools.partial(send, onward, zz, y, q, False, both, group))
                     if q is not third:
                         send(Y, zz, y, q, False, valid)
                     if q is first:
@@ -122,8 +130,8 @@
 
                 guarded(valid, body)
 
-    def take_y_own():
-        for q in (PAYLOAD, first, second, third, missing):
+    def take_y_own(quarters):
+        for q in quarters:
             arrived(index(z, other, core), q)
             send(CORE, z, other, q)
 
@@ -149,15 +157,24 @@
 
                 guarded(valid, body)
 
-    for step in range(1, nz + 2):
-        if step < nz:
-            take_z(step)
-        if step == 1:
-            take_y_own()
-        elif step - 1 < nz:
-            take_y(step - 1)
-        if 1 <= step - 2:
-            take_x(step - 2)
+    take_z(1, early)
+    take_z(2, early)
+    take_y_own((PAYLOAD, first, second))
+    take_y(1)
+    settle(paced)
+    send_z(third)
+    take_z(3, early)
+    take_y(2)
+    take_z(1, (third,))
+    take_x(1)
+    take_y(3)
+    send(Y, z, y, third, True)
+    send(Y, z, y, missing, True)
+    take_z(2, (third,))
+    take_x(2)
+    take_z(3, (third,))
+    take_y_own((third, missing))
+    take_x(3)
 
     for zz in range(nz):
         for yy in range(2):
@@ -165,8 +182,7 @@
                 arrived(index(zz, yy, 1 - core), q)
     for c in mine:
         c.wait()
-    for to, zz, yy, q, own, when in sent:
-        guarded(when, lambda: copy(to, zz, yy, q, own).wait_send())
+    settle(sent)
 
 
 def gather(coef, payload, wide):
@@ -193,142 +209,182 @@
 
 
 def product_kernel(
-    block, meta, pays_ref, coef_ref, full_ref, out_ref, half_ref, acc_ref, place, bra_of, start, fill
+    block, tiles, meta, pays_ref, coef_ref, full_ref, out_ref,
+    held, half_ref, acc_ref, ready, place, bra_of, start, fill, in_sem, out_sem,
 ):
+    wide, _, width = full_ref.shape
+
+    def load(w):
+        return pltpu.make_async_copy(full_ref.at[w], held.at[w], in_sem.at[w])
+
+    for w in range(wide):
+        load(w).start()
+
     slots = meta.shape[0] * 4
     places = place.shape[0]
 
-    @pl.when(pl.program_id(0) == 0)
-    def _():
-        def clear(i, _):
-            place[i] = -1
-            bra_of[i] = 0
-            return 0
-
-        lax.fori_loop(0, places, clear, 0)
-        for p in range(PAIR_COUNT):
-            fill[p] = 0
-
-        def count(s, _):
-            w, r = s // 4, s % 4
-
-            @pl.when(meta[w, 12 + r] > 0)
-            def _():
-                p = meta[w, r]
-                fill[p] = fill[p] + 1
-
-            return 0
-
-        lax.fori_loop(0, slots, count, 0)
-        start[0] = 0
-        for p in range(PAIR_COUNT):
-            start[p + 1] = start[p] + (fill[p] + 3) // 4
-            fill[p] = 4 * start[p]
-
-        def put(s, _):
-            w, r = s // 4, s % 4
-
-            @pl.when(meta[w, 12 + r] > 0)
-            def _():
-                p = meta[w, r]
-                to = fill[p]
-                place[to] = s
-                bra_of[to] = meta[w, 4 + r]
-                fill[p] = to + 1
-
-            return 0
-
-        lax.fori_loop(0, slots, put, 0)
-
-        def make(g, _):
-            parts = []
-            for k in range(4):
-                s = place[4 * g + k]
-                at = jnp.maximum(s, 0)
-                w, r = at // 4, at % 4
-                two = pays_ref[w, pl.ds(pl.multiple_of((r // 2) * block, block), block), :]
-                one = jnp.where(r % 2 == 0, two[:, :block], two[:, block:])
-                one = jnp.where(s >= 0, one, jnp.zeros_like(one))
-                ket = meta[w, 8 + r]
-                rows = coef_ref[pl.ds(pl.multiple_of(ket * block, block), block), :]
-                parts.append(jnp.dot(one, rows, preferred_element_type=jnp.float32))
-            half_ref[g] = jnp.concatenate(parts, axis=0).T.astype(jnp.bfloat16)
-            return 0
-
-        lax.fori_loop(0, start[PAIR_COUNT], make, 0)
-
-    tiles = full_ref.shape[0]
-    width = full_ref.shape[2]
-
-    def term(t, g):
+    def clear(i, _):
+        place[i] = -1
+        bra_of[i] = 0
+        return 0
+
+    lax.fori_loop(0, places, clear, 0)
+    for p in range(PAIR_COUNT):
+        fill[p] = 0
+
+    def count(s, _):
+        w, r = s // 4, s % 4
+
+        @pl.when(meta[w, 12 + r] > 0)
+        def _():
+            p = meta[w, r]
+            fill[p] = fill[p] + 1
+
+        return 0
+
+    lax.fori_loop(0, slots, count, 0)
+    start[0] = 0
+    for p in range(PAIR_COUNT):
+        start[p + 1] = start[p] + (fill[p] + 3) // 4
+        fill[p] = 4 * start[p]
+
+    def put(s, _):
+        w, r = s // 4, s % 4
+
+        @pl.when(meta[w, 12 + r] > 0)
+        def _():
+            p = meta[w, r]
+            to = fill[p]
+            place[to] = s
+            bra_of[to] = meta[w, 4 + r]
+            fill[p] = to + 1
+
+        return 0
+
+    lax.fori_loop(0, slots, put, 0)
+
+    def make(g, _):
+        parts = []
+        for k in range(4):
+            s = place[4 * g + k]
+            at = jnp.maximum(s, 0)
+            w, r = at // 4, at % 4
+            two = pays_ref[w, pl.ds(pl.multiple_of((r // 2) * block, block), block), :]
+            one = jnp.where(r % 2 == 0, two[:, :block], two[:, block:])
+            one = jnp.where(s >= 0, one, jnp.zeros_like(one))
+            ket = meta[w, 8 + r]
+            rows = coef_ref[pl.ds(pl.multiple_of(ket * block, block), block), :]
+            parts.append(jnp.dot(one, rows, preferred_element_type=jnp.float32))
+        half_ref[g] = jnp.concatenate(parts, axis=0).T.astype(jnp.bfloat16)
+        return 0
+
+    lax.fori_loop(0, start[PAIR_COUNT], make, 0)
+
+    span = tiles * width
+
+    def term(i, t, g):
         rows = [
-            full_ref[t, pl.ds(pl.multiple_of(bra_of[4 * g + k] * block, block), block), :]
+            held[i * tiles + t, pl.ds(pl.multiple_of(bra_of[4 * g + k] * block, block), block), :]
             for k in range(4)
         ]
         return jnp.dot(
             half_ref[g], jnp.concatenate(rows, axis=0), preferred_element_type=jnp.float32
         )
 
-    for p in range(PAIR_COUNT):
+    def store(i, slot, p):
+        columns = pl.ds(pl.multiple_of(i * span, span), span)
+        return pltpu.make_async_copy(
+            ready.at[slot, p], out_ref.at[p, :, columns], out_sem.at[slot, p]
+        )
+
+    def pair(i, slot, p):
         begin = start[p]
         groups = start[p + 1] - begin
 
         @pl.when(groups == 0)
         def _():
-            out_ref[p] = jnp.zeros(out_ref.shape[1:], out_ref.dtype)
+            ready[slot, p] = jnp.zeros(ready.shape[2:], ready.dtype)
 
         @pl.when(groups == 1)
         def _():
             for t in range(tiles):
-                out_ref[p, :, t * width : (t + 1) * width] = term(t, begin).astype(out_ref.dtype)
+                ready[slot, p, :, t * width : (t + 1) * width] = term(i, t, begin).astype(
+                    ready.dtype
+                )
 
         @pl.when(groups == 2)
         def _():
             for t in range(tiles):
-                out_ref[p, :, t * width : (t + 1) * width] = (
-                    term(t, begin) + term(t, begin + 1)
-                ).astype(out_ref.dtype)
+                ready[slot, p, :, t * width : (t + 1) * width] = (
+                    term(i, t, begin) + term(i, t, begin + 1)
+                ).astype(ready.dtype)
 
         @pl.when(groups > 2)
         def _():
             for t in range(tiles):
-                acc_ref[...] = term(t, begin)
-
-                def more(g, _, t=t):
-                    acc_ref[...] += term(t, g)
-                    return 0
-
-                lax.fori_loop(begin + 1, begin + groups, more, 0)
-                out_ref[p, :, t * width : (t + 1) * width] = acc_ref[...].astype(out_ref.dtype)
+                acc_ref[t] = term(i, t, begin) + term(i, t, begin + 1)
+
+            def more(g, _):
+                for t in range(tiles):
+                    acc_ref[t] += term(i, t, g)
+                return 0
+
+            lax.fori_loop(begin + 2, begin + groups, more, 0)
+            for t in range(tiles):
+                ready[slot, p, :, t * width : (t + 1) * width] = acc_ref[t].astype(ready.dtype)
+
+    count_of = wide // tiles
+
+    def strip(i, _):
+        slot = lax.rem(i, 2)
+        for t in range(tiles):
+            load(i * tiles + t).wait()
+
+        def one(p, _):
+            @pl.when(i >= 2)
+            def _():
+                store(i - 2, slot, p).wait()
+
+            pair(i, slot, p)
+            store(i, slot, p).start()
+            return 0
+
+        lax.fori_loop(0, PAIR_COUNT, one, 0)
+        return 0
+
+    lax.fori_loop(0, count_of, strip, 0)
+    for i in (count_of - 2, count_of - 1):
+        for p in range(PAIR_COUNT):
+            store(i, i % 2, p).wait()
 
 
 def product(meta, pays, coef, full, block):
     wide, rows, columns = full.shape
-    tiles = 2
+    tiles = 4
     most = wide + PAIR_COUNT
+    whole = pl.BlockSpec(memory_space=pltpu.VMEM)
     return pl.pallas_call(
-        functools.partial(product_kernel, block),
+        functools.partial(product_kernel, block, tiles),
         out_shape=jax.ShapeDtypeStruct((PAIR_COUNT, columns, wide * columns), jnp.bfloat16),
-        grid_spec=pltpu.PrefetchScalarGridSpec(
-            num_scalar_prefetch=1,
-            grid=(wide // tiles,),
-            in_specs=[
-                pl.BlockSpec(pays.shape, lambda i, m: (0, 0, 0)),
-                pl.BlockSpec(coef.shape, lambda i, m: (0, 0)),
-                pl.BlockSpec((tiles, rows, columns), lambda i, m: (i, 0, 0)),
-            ],
-            out_specs=pl.BlockSpec(
-                (PAIR_COUNT, columns, tiles * columns), lambda i, m: (0, 0, i)
-            ),
-            scratch_shapes=[
-                pltpu.VMEM((most, columns, 4 * block), jnp.bfloat16),
-                pltpu.VMEM((columns, columns), jnp.float32),
-                pltpu.SMEM((4 * most,), jnp.int32),
-                pltpu.SMEM((4 * most,), jnp.int32),
-                pltpu.SMEM((PAIR_COUNT + 1,), jnp.int32),
-                pltpu.SMEM((PAIR_COUNT,), jnp.int32),
-            ],
-        ),
+        in_specs=[
+            pl.BlockSpec(memory_space=pltpu.SMEM),
+            whole,
+            whole,
+            pl.BlockSpec(memory_space=pl.ANY),
+        ],
+        out_specs=pl.BlockSpec(memory_space=pl.ANY),
+        scratch_shapes=[
+            pltpu.VMEM(full.shape, full.dtype),
+            pltpu.VMEM((most, columns, 4 * block), jnp.bfloat16),
+            pltpu.VMEM((tiles, columns, columns), jnp.float32),
+            pltpu.VMEM((2, PAIR_COUNT, columns, tiles * columns), jnp.bfloat16),
+            pltpu.SMEM((4 * most,), jnp.int32),
+            pltpu.SMEM((4 * most,), jnp.int32),
+            pltpu.SMEM((PAIR_COUNT + 1,), jnp.int32),
+            pltpu.SMEM((PAIR_COUNT,), jnp.int32),
+            pltpu.SemaphoreType.DMA((wide,)),
+            pltpu.SemaphoreType.DMA((2, PAIR_COUNT)),
+        ],
         compiler_params=pltpu.CompilerParams(vmem_limit_bytes=48 * 1024 * 1024),
     )(meta, pays, coef, full)
 

time: 121 us -> 102 us (0.84)
  Pallas kernels: 115 us -> 95.1 us
    pallas_call x1, Pallas kernels: 86.5 us -> 74.6 us  [gather(): pl.pallas_call(functools.partial(gather_kernel, nz), out_shape=(jax.Shape...]
    pallas_call x1, Pallas kernels: 28.4 us -> 20.5 us  [product(): pl.pallas_call(functools.partial(product_kernel, block, tiles), out_shape...]
where the time goes in v2:
time: 102 us; the launch traced here: 101 us
  Pallas kernels  95.1 us (93%)
  local copies, waits for them, and re-layouts  3.48 us (3%)
  other arithmetic  2.1 us (2%)
    pallas_call x1, Pallas kernels, gather(): pl.pallas_call(functools.partial(gather_kernel, nz), out_shape=(jax.Shape...  74.6 us
    pallas_call x1, Pallas kernels, product(): pl.pallas_call(functools.partial(product_kernel, block, tiles), out_shape...  20.5 us
    unnamed x4, local copies, waits for them, and re-layouts  2.29 us

profile of v2, /device:TPU:1, one launch (start us, length us, event | category | flops | bytes accessed | tf_op | source)
XLA Modules:
  0.0 101.3 jit_solution(1286888023465250932)
XLA Ops:
  0.7 0.7 convert.7
  1.4 0.9 copy.13
  2.3 0.1 reshape.22
  2.4 0.6 pad_maximum_fusion.pay_ref
  3.0 74.6 %shard_map.46 = (bf16[16,2048,256]{2,1,0:T(8,128)(2,1)}, bf16[16,144,128]{2,1,0:T(8,128)(2,1)}) custom-call(bf16[2048,256]{1,0:T(8,128)(2,1)} %coef_ref.3, bf16[144,128]{1,0:T(8,128)(2,1)} %pad_maximum_fusion.pay_ref), custom_call_target="tpu_custom_call" | custom-call | bytes 33554432 | tf_op jit(solution)/shard_map/pallas_call | solution.py:191
  77.6 0.8 slice_convert_fusion
  78.3 0.1 copy.10
  78.4 0.1 copy.11.meta
  78.5 0.0 copy-start
  78.5 1.2 %copy-done = bf16[2048,256]{1,0:T(8,128)(2,1)S(1)} copy-done((bf16[2048,256]{1,0:T(8,128)(2,1)S(1)}, bf16[2048,256]{1,0:T(8,128)(2,1)}, u32[]{:S(2)}) %copy-start) | copy-done | bytes 1048600
  79.7 0.0 copy-start.1
  79.7 1.1 %copy-done.1 = bf16[16,144,128]{2,1,0:T(8,128)(2,1)S(1)} copy-done((bf16[16,144,128]{2,1,0:T(8,128)(2,1)S(1)}, bf16[16,144,128]{2,1,0:T(8,128)(2,1)}, u32[]{:S(2)}) %copy-start.1) | copy-done | bytes 589848
  80.8 20.5 %shard_map.47 = bf16[8,256,4096]{2,1,0:T(8,128)(2,1)} custom-call(s32[16,16]{1,0:T(8,128)S(1)} %copy.11.meta, bf16[16,144,128]{2,1,0:T(8,128)(2,1)S(1)} %copy-done.1, bf16[2048,256]{1,0:T(8,128)(2,1)S(1)} %copy-done, bf16[16,2048,256]{2,1,0:T(8,128)(2,1)} %get-tuple-element.8.full_ref), custom_call_target="tpu_custom_call" | custom-call | tf_op jit(solution)/shard_map/pallas_call | solution.py:366
  (2 shorter events, 0.0 us)
Async XLA Ops:
  78.5 1.2 %copy-start = (bf16[2048,256]{1,0:T(8,128)(2,1)S(1)}, bf16[2048,256]{1,0:T(8,128)(2,1)}, u32[]{:S(2)}) copy-start(bf16[2048,256]{1,0:T(8,128)(2,1)} %coef_ref.3) | copy-start | bytes 3145732
  79.7 1.1 %copy-start.1 = (bf16[16,144,128]{2,1,0:T(8,128)(2,1)S(1)}, bf16[16,144,128]{2,1,0:T(8,128)(2,1)}, u32[]{:S(2)}) copy-start(bf16[16,144,128]{2,1,0:T(8,128)(2,1)} %get-tuple-element.7.pays_ref) | copy-start | bytes 1769476

commit v3 on v2

--- a/solution.py
+++ b/solution.py
@@ -360,7 +360,7 @@
 
 def product(meta, pays, coef, full, block):
     wide, rows, columns = full.shape
-    tiles = 4
+    tiles = 8
     most = wide + PAIR_COUNT
     whole = pl.BlockSpec(memory_space=pltpu.VMEM)
     return pl.pallas_call(

time: 102 us -> 98.6 us (0.967)
  Pallas kernels: 95.1 us -> 92.4 us
    pallas_call x1, Pallas kernels: 20.5 us -> 17.9 us  [product(): pl.pallas_call(functools.partial(product_kernel, block, tiles), out_shape...]
where the time goes in v3:
time: 98.6 us; the launch traced here: 98.7 us
  Pallas kernels  92.4 us (94%)
  local copies, waits for them, and re-layouts  3.48 us (4%)
  other arithmetic  2.1 us (2%)
    pallas_call x1, Pallas kernels, gather(): pl.pallas_call(functools.partial(gather_kernel, nz), out_shape=(jax.Shape...  74.6 us
    pallas_call x1, Pallas kernels, product(): pl.pallas_call(functools.partial(product_kernel, block, tiles), out_shape...  17.9 us
    unnamed x4, local copies, waits for them, and re-layouts  2.29 us

profile of v3, /device:TPU:1, one launch (start us, length us, event | category | flops | bytes accessed | tf_op | source)
XLA Modules:
  0.0 98.7 jit_solution(18140987201093305826)
XLA Ops:
  0.7 0.7 convert.7
  1.4 0.9 copy.13
  2.3 0.1 reshape.22
  2.4 0.6 pad_maximum_fusion.pay_ref
  3.0 74.6 %shard_map.46 = (bf16[16,2048,256]{2,1,0:T(8,128)(2,1)}, bf16[16,144,128]{2,1,0:T(8,128)(2,1)}) custom-call(bf16[2048,256]{1,0:T(8,128)(2,1)} %coef_ref.3, bf16[144,128]{1,0:T(8,128)(2,1)} %pad_maximum_fusion.pay_ref), custom_call_target="tpu_custom_call" | custom-call | bytes 33554432 | tf_op jit(solution)/shard_map/pallas_call | solution.py:191
  77.6 0.8 slice_convert_fusion
  78.3 0.1 copy.10
  78.4 0.1 copy.11.meta
  78.5 0.0 copy-start
  78.5 1.2 %copy-done = bf16[2048,256]{1,0:T(8,128)(2,1)S(1)} copy-done((bf16[2048,256]{1,0:T(8,128)(2,1)S(1)}, bf16[2048,256]{1,0:T(8,128)(2,1)}, u32[]{:S(2)}) %copy-start) | copy-done | bytes 1048600
  79.7 0.0 copy-start.1
  79.7 1.1 %copy-done.1 = bf16[16,144,128]{2,1,0:T(8,128)(2,1)S(1)} copy-done((bf16[16,144,128]{2,1,0:T(8,128)(2,1)S(1)}, bf16[16,144,128]{2,1,0:T(8,128)(2,1)}, u32[]{:S(2)}) %copy-start.1) | copy-done | bytes 589848
  80.8 17.9 %shard_map.47 = bf16[8,256,4096]{2,1,0:T(8,128)(2,1)} custom-call(s32[16,16]{1,0:T(8,128)S(1)} %copy.11.meta, bf16[16,144,128]{2,1,0:T(8,128)(2,1)S(1)} %copy-done.1, bf16[2048,256]{1,0:T(8,128)(2,1)S(1)} %copy-done, bf16[16,2048,256]{2,1,0:T(8,128)(2,1)} %get-tuple-element.8.full_ref), custom_call_target="tpu_custom_call" | custom-call | tf_op jit(solution)/shard_map/pallas_call | solution.py:366
  (2 shorter events, 0.0 us)
Async XLA Ops:
  78.5 1.2 %copy-start = (bf16[2048,256]{1,0:T(8,128)(2,1)S(1)}, bf16[2048,256]{1,0:T(8,128)(2,1)}, u32[]{:S(2)}) copy-start(bf16[2048,256]{1,0:T(8,128)(2,1)} %coef_ref.3) | copy-start | bytes 3145732
  79.7 1.1 %copy-start.1 = (bf16[16,144,128]{2,1,0:T(8,128)(2,1)S(1)}, bf16[16,144,128]{2,1,0:T(8,128)(2,1)}, u32[]{:S(2)}) copy-start(bf16[16,144,128]{2,1,0:T(8,128)(2,1)} %get-tuple-element.7.pays_ref) | copy-start | bytes 1769476
